TPU v7x, 32 devices: a whole 2x2x4 slice. The times are simulated.
32 devices in a mesh: groups: 2 (over y), pool: 8 (over z, x), tensor: 2 (over core).
Axes of the slice: x: 2, y: 2, z: 4, core: 2. Of those that a mesh axis runs over, the one named last changes fastest.
Arguments:
- queries: bfloat16 [2, 16, 128, 4096], P(None, ('groups', 'pool'), None, 'tensor'), parts along dimension 1, may hold values from -140 to 140
- new_kv: bfloat16 [2, 16, 128, 1024], P(None, ('groups', 'pool'), None, 'tensor'), parts along dimension 1, may hold values from -6 to 6
- store: bfloat16 [2, 1024, 64, 1024], P(None, ('groups', 'pool'), None, 'tensor'), parts along dimension 1, may hold values from -6 to 6
- fetch_list: int32 [2, 16, 64, 2], P(None, 'groups'), parts along dimension 1, may hold values from 0 to 63, as said below
- prefix_blocks: int32 [16], P('groups'), parts along dimension 0, may hold values from 1 to 64, 204 in all
- writeback_map: int32 [2, 16, 2, 2], P(None, 'groups'), parts along dimension 1, may hold values from 0 to 7, as said below
Outputs:
- attention: bfloat16 [2, 16, 128, 4096], P(None, ('groups', 'pool'), None, 'tensor'), parts along dimension 1
- written: bfloat16 [2, 64, 64, 1024], P(None, ('groups', 'pool'), None, 'tensor'), parts along dimension 1
There are 2 independent parts, one for each index of `groups`. A program takes and returns all parts, laid end to end along the dimension named above; each array names one. Nothing has to cross between parts.
Inputs may be any that keep to these rules, and one draw needn't show every extreme that they name: `fetch_list`: entry j of a session's list at a layer is used only where j is below the session's prefix_blocks. The used entries of one session name at most 8 blocks of one owner, and in every draw some session names exactly 8 of some owner. No two used entries of one layer name the same owner and slot. `writeback_map`: at each layer the 2 new blocks of session s go to distinct owners (s + (d mod 2) + (d div 2) * 2 * 2) mod 8 with 0 <= d < 4, each into slot d of that owner; in every layer some owner receives exactly 4 new blocks.
All inputs are finite; a program needn't handle non-finite values.
Results may differ from a plain program's by a relative error of at most 0.0071.
Values may be sent and summed in bfloat16 or wider, within the bound.
A program may use at most 192 MiB of HBM per device.

v0:
```python
import functools

import jax
import jax.numpy as jnp
from jax import lax
from jax.experimental import pallas as pl
from jax.experimental.pallas import tpu as pltpu
from jax.sharding import PartitionSpec as P

HD = 128
GROUP = 8
MAXB = 64
NBNEW = 2
WSLOTS = 4


def rotate(source, places):
    half_width = source.shape[-1] // 2
    frequencies = 500000.0 ** (
        -(jnp.arange(half_width, dtype=jnp.float32) * 2.0 / source.shape[-1])
    )
    angles = places[..., None] * frequencies
    cosine = jnp.cos(angles)
    sine_part = jnp.sin(angles)
    first_half = source[..., :half_width]
    second = source[..., half_width:]
    return jnp.concatenate(
        [first_half * cosine - second * sine_part, second * cosine + first_half * sine_part], -1
    )


def per_device(queries, new_kv, store, fetch_list, prefix_blocks, writeback_map):
    pool_size = lax.axis_size("pool")
    my_index = lax.axis_index("pool")
    layer_count = queries.shape[0]
    new_count = queries.shape[2]
    block_len = store.shape[2]
    row_width = store.shape[3]
    kv_local = row_width // (2 * HD)
    per_owner = MAXB // pool_size
    score_scale = HD ** (-0.5)
    length = prefix_blocks[my_index]
    places = (length * block_len + jnp.arange(new_count, dtype=jnp.int32)).astype(jnp.float32)
    block_order = jnp.arange(MAXB, dtype=jnp.int32)
    earlier = block_order[None, :] < block_order[:, None]
    live_entries = block_order[None, :] < prefix_blocks[:, None]
    lane_ids = jnp.arange(per_owner, dtype=jnp.int32)
    sources = jnp.arange(pool_size, dtype=jnp.int32)
    slot_range = jnp.arange(WSLOTS, dtype=jnp.int32)
    token_ids = jnp.arange(new_count, dtype=jnp.int32)
    causal_rows = jnp.repeat(token_ids[None, :] <= token_ids[:, None], GROUP, axis=0)
    attention_all = []
    written_all = []
    for layer_index in range(layer_count):
        owners = fetch_list[layer_index, :, :, 0]
        slot_ids = fetch_list[layer_index, :, :, 1]
        owner_rank = jnp.sum((owners[:, :, None] == owners[:, None, :]) & earlier[None], -1)
        chosen = ((owners == my_index) & live_entries)[:, None, :] & (
            owner_rank[:, None, :] == lane_ids[None, :, None]
        )
        picked = jnp.sum(jnp.where(chosen, slot_ids[:, None, :], 0), -1).reshape(-1)
        present = jnp.any(chosen, -1).reshape(-1)
        picked_rows = jnp.take(store[layer_index], picked, axis=0)
        outgoing = jnp.where(present[:, None, None], picked_rows, jnp.zeros_like(picked_rows))
        arrival = (
            (owners[my_index][:, None, None] == sources[None, :, None])
            & (owner_rank[my_index][:, None, None] == lane_ids[None, None, :])
            & live_entries[my_index][:, None, None]
        )
        outgoing, prefix_ok = (outgoing, jnp.any(arrival, 0).reshape(-1))
        prefix = lax.all_to_all(outgoing, "pool", split_axis=0, concat_axis=0, tiled=True)
        rotated_query = rotate(
            queries[layer_index, 0].reshape(new_count, kv_local, GROUP, HD).astype(jnp.float32),
            places[:, None, None],
        ).astype(jnp.bfloat16)
        fresh_rows = new_kv[layer_index, 0].reshape(new_count, kv_local, 2, HD)
        new_keys = rotate(fresh_rows[:, :, 0].astype(jnp.float32), places[:, None]).astype(
            jnp.bfloat16
        )
        values = fresh_rows[:, :, 1]
        key_count = prefix.shape[0] * prefix.shape[1]
        flat_prefix = prefix.reshape(key_count, kv_local, 2, HD)
        kept_keys = jnp.repeat(prefix_ok, prefix.shape[1])
        results = []
        for head_index in range(kv_local):
            query_rows = rotated_query[:, head_index].reshape(new_count * GROUP, HD)
            far_scores = (
                jnp.einsum(
                    "rd,nd->rn",
                    query_rows,
                    flat_prefix[:, head_index, 0],
                    preferred_element_type=jnp.float32,
                )
                * score_scale
            )
            near_scores = (
                jnp.einsum(
                    "rd,nd->rn",
                    query_rows,
                    new_keys[:, head_index],
                    preferred_element_type=jnp.float32,
                )
                * score_scale
            )
            far_scores = jnp.where(kept_keys[None, :], far_scores, -jnp.inf)
            near_scores = jnp.where(causal_rows, near_scores, -jnp.inf)
            row_top = jnp.maximum(jnp.max(far_scores, -1), jnp.max(near_scores, -1))
            far_weights = jnp.exp(far_scores - row_top[:, None])
            near_weights = jnp.exp(near_scores - row_top[:, None])
            row_total = jnp.sum(far_weights, -1) + jnp.sum(near_weights, -1)
            mixture = jnp.einsum(
                "rn,nd->rd",
                far_weights.astype(jnp.bfloat16),
                flat_prefix[:, head_index, 1],
                preferred_element_type=jnp.float32,
            )
            mixture = mixture + jnp.einsum(
                "rn,nd->rd",
                near_weights.astype(jnp.bfloat16),
                values[:, head_index],
                preferred_element_type=jnp.float32,
            )
            results.append((mixture / row_total[:, None]).reshape(new_count, GROUP, HD))
        attention = (
            jnp.stack(results, 1).reshape(new_count, kv_local * GROUP * HD).astype(jnp.bfloat16)
        )
        attend_blocks = jnp.stack([new_keys, values], 2).reshape(NBNEW, block_len * row_width)
        attention, blocks = (attention, attend_blocks)
        attention_all.append(attention)
        targets = writeback_map[layer_index, :, :, 0]
        target_slots = writeback_map[layer_index, :, :, 1]
        flat_targets = targets.reshape(-1)
        flat_slots = target_slots.reshape(-1)
        selector = (
            (flat_targets == my_index)[None, :] & (flat_slots[None, :] == slot_range[:, None])
        ).astype(jnp.bfloat16)
        stored = jnp.dot(
            selector,
            lax.all_gather(blocks, "pool", axis=0, tiled=True),
            preferred_element_type=jnp.float32,
        )
        written_all.append(stored.astype(jnp.bfloat16).reshape(WSLOTS, block_len, row_width))
    return (jnp.stack(attention_all)[:, None], jnp.stack(written_all))

EMPTY = -1e30
EXP_SCALE = HD ** (-0.5) * 1.4426950408889634
MASKED = -2e30


def gather_kernel(picks, store_ref, out_ref, sems):
    count = out_ref.shape[0]

    def copy(i):
        return pltpu.make_async_copy(store_ref.at[picks[i]], out_ref.at[i], sems.at[i])

    lax.fori_loop(0, count, lambda i, x: (copy(i).start(), x)[1], 0)
    lax.fori_loop(0, count, lambda i, x: (copy(i).wait(), x)[1], 0)


def gather_blocks(picks, flat_store):
    return pl.pallas_call(
        gather_kernel,
        out_shape=jax.ShapeDtypeStruct(picks.shape + flat_store.shape[1:], flat_store.dtype),
        grid_spec=pltpu.PrefetchScalarGridSpec(
            num_scalar_prefetch=1,
            grid=(),
            in_specs=[pl.BlockSpec(memory_space=pl.ANY)],
            out_specs=pl.BlockSpec(memory_space=pl.ANY),
            scratch_shapes=[pltpu.SemaphoreType.DMA(picks.shape)],
        ),
    )(picks, flat_store)


def shift_of(d, pool_size):
    return d % 2 + d // 2 * (2 * pool_size // WSLOTS)


def pair_kernel(
    pool_size, block_len, counts, q_ref, sent_ref, local_ref, new_ref, back_ref,
    out_ref, written_ref,
    q_all, other, part, stat, low, low_stat, high, high_stat, landed,
    kv_send, kv_recv, q_send, q_recv, p_send, p_recv, w_send, w_recv,
):
    pairs = pool_size // 2
    layers, heads, rows, _ = q_ref.shape
    new_count = new_ref.shape[1]
    kept = local_ref.shape[2]
    me = lax.axis_index("pool")
    line = me // 2
    partner = me + 1 - 2 * (me % 2)

    def remote(src, dst, send, recv, device):
        return pltpu.make_async_remote_copy(
            src_ref=src, dst_ref=dst, send_sem=send, recv_sem=recv,
            device_id={"pool": device}, device_id_type=pl.DeviceIdType.MESH,
        )

    barrier = pltpu.get_barrier_semaphore()
    for k in range(1, pool_size):
        pl.semaphore_signal(
            barrier, inc=1, device_id={"pool": lax.rem(me + k, pool_size)},
            device_id_type=pl.DeviceIdType.MESH,
        )
    pl.semaphore_wait(barrier, pool_size - 1)

    def kv_copy(l, t):
        return remote(
            sent_ref.at[l, t], other.at[l, t], kv_send.at[l, t], kv_recv.at[l, t], partner
        )

    def q_down(l, step):
        src = q_ref.at[l] if step == 1 else q_all.at[l, step - 1]
        return remote(
            src, q_all.at[l, step], q_send.at[l, 0, step], q_recv.at[l, step],
            lax.rem(me + pool_size - 2, pool_size),
        )

    def q_up(l, step):
        src = q_ref.at[l] if step == 1 else q_all.at[l, pairs - step + 1]
        return remote(
            src, q_all.at[l, pairs - step], q_send.at[l, 1, step], q_recv.at[l, pairs - step],
            lax.rem(me + 2, pool_size),
        )

    def goes_down(step):
        return (line >= 1) & (line + step <= pairs)

    def goes_up(step):
        return (line <= pairs - 2) & (line - step + 1 >= 0)

    def back_copy(d):
        device = lax.rem(me + shift_of(d, pool_size), pool_size)
        return remote(back_ref.at[d], landed.at[d], w_send.at[d], w_recv.at[d], device)

    def q_step(l, step):
        @pl.when(goes_down(step))
        def _():
            if step > 1:
                q_down(l, step - 1).wait_recv()
            q_down(l, step).start()

        @pl.when(goes_up(step))
        def _():
            if step > 1:
                q_up(l, step - 1).wait_recv()
            q_up(l, step).start()

    def wait_query(l, t):
        from_above = line + t <= pairs - 1
        passed = jnp.where(from_above, goes_down(t + 1), goes_up(pairs - t + 1))

        @pl.when(jnp.logical_not(passed))
        def _():
            q_down(l, t).wait_recv()

    def attend(l, t, near):
        def one_head(h, carry):
            q = q_ref[l, h] if near else q_all[l, t, h]
            cols = pl.ds(pl.multiple_of(h * 2 * HD, 2 * HD), HD)
            value_cols = pl.ds(pl.multiple_of(h * 2 * HD + HD, HD), HD)

            def add(state, k, v, keep):
                old, total, acc = state
                s = lax.dot_general(
                    k, q, (((1,), (1,)), ((), ())), preferred_element_type=jnp.float32
                )
                s = jnp.where(keep(s.shape), s, MASKED)
                fresh = jnp.maximum(old, jnp.max(s, 0, keepdims=True))
                p = jnp.exp2((s - fresh) * EXP_SCALE)
                fade = jnp.exp2((old - fresh) * EXP_SCALE)
                total = total * fade + jnp.sum(p, 0, keepdims=True)
                acc = acc * fade + lax.dot_general(
                    v, p.astype(jnp.bfloat16), (((0,), (0,)), ((), ())),
                    preferred_element_type=jnp.float32,
                )
                return fresh, total, acc

            state = (
                jnp.full((1, rows), EMPTY, jnp.float32),
                jnp.zeros((1, rows), jnp.float32),
                jnp.zeros((HD, rows), jnp.float32),
            )
            if near:
                def causal(shape):
                    token = lax.broadcasted_iota(jnp.int32, shape, 1) % new_count
                    return lax.broadcasted_iota(jnp.int32, shape, 0) <= token

                state = add(state, new_ref[l, :, cols], new_ref[l, :, value_cols], causal)
            for which, ref in ((0, local_ref), (1, other)):
                length = counts[l, which, t] * block_len
                state = add(
                    state, ref[l, t, :, cols], ref[l, t, :, value_cols],
                    lambda shape: lax.broadcasted_iota(jnp.int32, shape, 0) < length,
                )
            part[l, t, h] = state[2].astype(jnp.bfloat16)
            stat[l, t, h, 0:1] = state[0]
            stat[l, t, h, 1:2] = state[1]
            return carry

        lax.fori_loop(0, heads, one_head, 0)

    def p_copies(l, step, up):
        t = pairs - step if up else step
        lands, stats = (high, high_stat) if up else (low, low_stat)
        device = lax.rem(me + 2 if up else me + pool_size - 2, pool_size)
        side = int(up)
        return (
            remote(part.at[l, t], lands.at[l, step], p_send.at[l, side, step, 0],
                   p_recv.at[l, side, step, 0], device),
            remote(stat.at[l, t], stats.at[l, step], p_send.at[l, side, step, 1],
                   p_recv.at[l, side, step, 1], device),
        )

    def p_wait(l, step, up):
        for copy in p_copies(l, step, up):
            copy.wait_recv()

    def fold(l, t, step, up):
        lands, stats = (high, high_stat) if up else (low, low_stat)
        for h in range(heads):
            mine, theirs = stat[l, t, h, 0:1], stats[l, step, h, 0:1]
            top = jnp.maximum(mine, theirs)
            a, b = jnp.exp2((mine - top) * EXP_SCALE), jnp.exp2((theirs - top) * EXP_SCALE)
            part[l, t, h] = (
                part[l, t, h].astype(jnp.float32) * a + lands[l, step, h].astype(jnp.float32) * b
            ).astype(jnp.bfloat16)
            stat[l, t, h, 0:1] = top
            stat[l, t, h, 1:2] = stat[l, t, h, 1:2] * a + stats[l, step, h, 1:2] * b

    def sends(step, up):
        return line < step if up else line + step >= pairs

    def has_source(up):
        return line >= 1 if up else line <= pairs - 2

    def p_step(l, step):
        for up in (False, True):
            t = pairs - step if up else step

            @pl.when(sends(step, up))
            def _(up=up, t=t):
                if step > 1:
                    @pl.when(has_source(up))
                    def _():
                        p_wait(l, step - 1, up)
                        fold(l, t, step - 1, up)
                for copy in p_copies(l, step, up):
                    copy.start()

    def finish(l):
        for up in (False, True):
            @pl.when(has_source(up))
            def _(up=up):
                p_wait(l, pairs - 1, up)
                fold(l, 0, pairs - 1, up)
        for h in range(heads):
            done = part[l, 0, h].astype(jnp.float32) / stat[l, 0, h, 1:2]
            for g in range(GROUP):
                piece = done[:, g * new_count : (g + 1) * new_count].T
                first = (h * GROUP + g) * HD
                out_ref[l, :, first : first + HD] = piece.astype(jnp.bfloat16)

    order = [1, 3, 2]
    q_step(0, 1)
    for l in range(layers):
        kv_copy(l, 0).start()
    q_step(1, 1)
    for l in range(layers):
        for t in order:
            kv_copy(l, t).start()
    for d in range(1, WSLOTS):
        back_copy(d).start()
    kv_copy(0, 0).wait_recv()
    attend(0, 0, True)
    q_step(0, 2)
    kv_copy(1, 0).wait_recv()
    attend(1, 0, True)
    q_step(0, 3)
    q_step(1, 2)
    for n, t in enumerate(order):
        kv_copy(0, t).wait_recv()
        wait_query(0, t)
        attend(0, t, False)
        if n == 0:
            q_step(1, 3)
    p_step(0, 1)
    for n, t in enumerate(order):
        kv_copy(1, t).wait_recv()
        wait_query(1, t)
        attend(1, t, False)
        if n < 2:
            p_step(0, n + 2)
    p_step(1, 1)
    finish(0)
    for step in range(2, pairs):
        p_step(1, step)
    for d in range(WSLOTS):
        if d:
            back_copy(d).wait_recv()
        for l in range(layers):
            written_ref[l, d] = landed[d, l] if d else back_ref[d, l]
    finish(1)
    for l in range(layers):
        for t in range(pairs):
            kv_copy(l, t).wait_send()
        for step in range(1, pairs):
            pl.when(goes_down(step))(lambda: q_down(l, step).wait_send())
            pl.when(goes_up(step))(lambda: q_up(l, step).wait_send())
            for up in (False, True):
                @pl.when(sends(step, up))
                def _(up=up):
                    for copy in p_copies(l, step, up):
                        copy.wait_send()
    for d in range(1, WSLOTS):
        back_copy(d).wait_send()


def pair_attention(pool_size, block_len, counts, asked, sent, local, new_rows, back):
    layers, heads, rows, _ = asked.shape
    pairs = pool_size // 2
    new_count = new_rows.shape[1]
    vmem = pl.BlockSpec(memory_space=pltpu.VMEM)
    dma = pltpu.SemaphoreType.DMA
    sums = pltpu.VMEM((layers, pairs, heads, HD, rows), jnp.bfloat16)
    stats = pltpu.VMEM((layers, pairs, heads, 8, rows), jnp.float32)
    return pl.pallas_call(
        functools.partial(pair_kernel, pool_size, block_len),
        out_shape=(
            jax.ShapeDtypeStruct((layers, new_count, heads * GROUP * HD), jnp.bfloat16),
            jax.ShapeDtypeStruct((layers, WSLOTS) + back.shape[2:], jnp.bfloat16),
        ),
        in_specs=[pl.BlockSpec(memory_space=pltpu.SMEM), vmem,
                  pl.BlockSpec(memory_space=pl.ANY), vmem, vmem, vmem],
        out_specs=(vmem, vmem),
        scratch_shapes=[
            pltpu.VMEM((layers, pairs, heads, rows, HD), jnp.bfloat16),
            pltpu.VMEM(local.shape, jnp.bfloat16),
            sums, stats, sums, stats, sums, stats,
            pltpu.VMEM(back.shape, jnp.bfloat16),
            dma((layers, pairs)), dma((layers, pairs)),
            dma((layers, 2, pairs)), dma((layers, pairs)),
            dma((layers, 2, pairs, 2)), dma((layers, 2, pairs, 2)),
            dma((WSLOTS,)), dma((WSLOTS,)),
        ],
        compiler_params=pltpu.CompilerParams(
            collective_id=0, has_side_effects=True, vmem_limit_bytes=56 * 1024 * 1024
        ),
    )(counts, asked, sent, local, new_rows, back)


def per_device_rows(pool_size, queries, new_kv, store, fetch_list, prefix_blocks, writeback_map):
    pair_count = pool_size // 2
    me = lax.axis_index("pool")
    line, side = me // 2, me % 2
    layers, _, new_count, _ = queries.shape
    sessions = prefix_blocks.shape[0]
    slots, block_len, row_width = store.shape[1:]
    heads = row_width // (2 * HD)
    cap = MAXB // pool_size

    length = prefix_blocks[me]
    places = (length * block_len + jnp.arange(new_count, dtype=jnp.int32)).astype(jnp.float32)
    asked = []
    for layer in range(layers):
        turned = rotate(
            queries[layer, 0].reshape(new_count, heads, GROUP, HD).astype(jnp.float32),
            places[:, None, None],
        ).astype(jnp.bfloat16)
        asked.append(turned.transpose(1, 2, 0, 3).reshape(heads, GROUP * new_count, HD))

    live = jnp.arange(MAXB, dtype=jnp.int32)[None, :] < prefix_blocks[:, None]
    earlier = jnp.triu(jnp.ones((MAXB, MAXB), jnp.float32), 1)

    def used(owner):
        return (fetch_list[..., 0] == owner) & live[None]

    mine = used(me)
    rank = jnp.dot(mine.astype(jnp.float32), earlier).astype(jnp.int32)
    lanes = jnp.arange(cap, dtype=jnp.int32)
    chosen = mine[:, :, None, :] & (rank[:, :, None, :] == lanes[:, None])
    picked = jnp.sum(jnp.where(chosen, fetch_list[:, :, None, :, 1], 0), -1)
    picked = picked + (jnp.arange(layers, dtype=jnp.int32) * slots)[:, None, None]
    picked = picked.reshape(layers, pair_count, 2, cap)
    by_side = lambda a: jnp.sum(a.astype(jnp.int32), -1).reshape(layers, pair_count, 2)
    turned_lines = (line + jnp.arange(pair_count, dtype=jnp.int32)) % pair_count

    def ours(a, which):
        return jnp.take(lax.dynamic_index_in_dim(a, which, 2, False), turned_lines, axis=1)

    counts = jnp.stack(
        [ours(by_side(mine), side), ours(by_side(used(me + 1 - 2 * side)), side)], 1
    )
    flat_store = store.reshape(layers * slots, block_len, row_width)
    held = (layers, pair_count, cap * block_len, row_width)
    sent = gather_blocks(ours(picked, 1 - side).reshape(-1), flat_store).reshape(held)
    local = gather_blocks(ours(picked, side).reshape(-1), flat_store).reshape(held)
    fresh = new_kv[:, 0].reshape(layers, new_count, heads, 2, HD)
    new_keys = rotate(fresh[:, :, :, 0].astype(jnp.float32), places[:, None]).astype(jnp.bfloat16)
    new_rows = jnp.stack([new_keys, fresh[:, :, :, 1]], 3).reshape(layers, new_count, row_width)

    new_blocks = new_rows.reshape(layers, NBNEW, block_len, row_width)
    slot_of = writeback_map[:, me, :, 1]
    back = []
    for d in range(WSLOTS):
        block = jnp.zeros((layers, block_len, row_width), jnp.bfloat16)
        for b in range(NBNEW):
            block = jnp.where((slot_of[:, b] == d)[:, None, None], new_blocks[:, b], block)
        back.append(block)
    attention, written = pair_attention(
        pool_size, block_len, counts, jnp.stack(asked), sent, local, new_rows, jnp.stack(back)
    )
    return attention[:, None], written


def solution(mesh):
    pool_size = mesh.shape["pool"]
    if pool_size == 8:
        plan = functools.partial(per_device_rows, pool_size)
    else:
        plan = per_device
    in_specs = (
        P(None, ("groups", "pool"), None, "tensor"),
        P(None, ("groups", "pool"), None, "tensor"),
        P(None, ("groups", "pool"), None, "tensor"),
        P(None, "groups", None, None),
        P("groups"),
        P(None, "groups", None, None),
    )
    out_specs = (
        P(None, ("groups", "pool"), None, "tensor"),
        P(None, ("groups", "pool"), None, "tensor"),
    )
    return jax.shard_map(
        plan, mesh=mesh, in_specs=in_specs, out_specs=out_specs, check_vma=False
    )
```

profile of v0, /device:TPU:8, one launch (start us, length us, event | category | flops | bytes accessed | tf_op | source)
XLA Modules:
  0.0 440.4 jit_solution(5062599455184692598)
XLA Ops:
  0.7 1.3 dynamic_slice.22
  2.7 0.2 dynamic-slice_reduce_fusion
  3.0 0.7 iota_compare_fusion.3
  3.7 0.3 compare_reduce_fusion.7
  4.0 0.8 fusion.12
  4.8 0.1 convert_reduce_fusion.1
  5.0 0.1 reshape.395
  5.0 0.1 reshape.396
  5.1 0.1 constant_dynamic-slice_fusion.2
  5.2 0.1 copy.62
  5.3 0.6 gather_fusion.1
  5.9 0.1 copy.59
  6.0 0.6 gather_fusion
  6.6 0.1 select_bitcast_fusion.3
  6.6 0.1 copy.45
  6.7 0.1 copy.46
  6.8 0.6 pad_add_fusion.counts
  7.4 0.1 convolution_convert_fusion
  7.5 0.4 select_reduce_fusion
  8.0 0.6 gather_fusion.3
  8.6 0.6 gather_fusion.2
  9.1 0.1 select_bitcast_fusion
  9.2 0.6 reshape.400.picks
  9.8 0.6 reshape.397.picks
  10.4 0.3 multiply_cosine_fusion
  10.7 1.0 reshape_squeeze.2
  11.8 0.4 slice_convert_fusion
  12.1 0.5 fusion
  12.6 0.4 pad_maximum_fusion.5
  12.9 0.3 copy.55
  13.2 0.6 pad_maximum_fusion.4
  13.8 0.1 reshape_reshape.3
  13.9 0.8 reshape.402.new_ref
  14.8 0.1 select_select_fusion.3
  14.9 0.9 pad_maximum_fusion.3.back_ref
  15.8 0.2 convert_bitcast_fusion.1
  16.0 0.2 copy.72
  16.2 0.2 copy.73
  16.4 0.3 fusion.11
  16.7 0.3 fusion.10
  17.1 1.4 subtract_convert_fusion.1
  18.5 0.6 pad_maximum_fusion.1
  19.1 1.1 pad_maximum_fusion.q_ref
  20.1 129.6 %shard_map.77 = bf16[64,64,512]{2,1,0:T(8,128)(2,1)} custom-call(s32[64]{0:T(128)} %reshape.397.picks, bf16[128,64,512]{2,1,0:T(8,128)(2,1)} %bitcast.86), custom_call_target="tpu_custom_call" | custom-call | tf_op jit(solution)/shard_map/pallas_call | solution.py:161
  149.7 129.4 %shard_map.78 = bf16[64,64,512]{2,1,0:T(8,128)(2,1)} custom-call(s32[64]{0:T(128)} %reshape.400.picks, bf16[128,64,512]{2,1,0:T(8,128)(2,1)} %bitcast.87), custom_call_target="tpu_custom_call" | custom-call | tf_op jit(solution)/shard_map/pallas_call | solution.py:161
  279.1 157.1 %shard_map.79 = (bf16[2,128,2048]{2,1,0:T(8,128)(2,1)}, bf16[2,4,64,512]{3,2,1,0:T(8,128)(2,1)}) custom-call(s32[2,2,4]{2,1,0:T(2,128)} %pad_add_fusion.counts, bf16[2,2,1024,128]{3,2,1,0:T(8,128)(2,1)} %pad_maximum_fusion.q_ref, bf16[2,4,512,512]{3,2,1,0:T(8,128)(2,1)} %bitcast.88, bf16[2,4,512,512]{3,2,1,0:T(8,128)(2,1)} %bitcast.89, ...), custom_call_target="tpu_custom_call" | custom-call | tf_op jit(solution)/shard_map/pallas_call | solution.py:426
  436.3 2.3 copy.84
  438.6 1.9 copy.85
  (16 shorter events, 0.2 us)
Async XLA Ops:
  0.6 2.1 copy-start
  0.6 15.1 %copy-start.1 = (bf16[2,1,128,2048]{3,2,1,0:T(8,128)(2,1)S(1)}, bf16[2,1,128,2048]{3,2,1,0:T(8,128)(2,1)}, u32[]{:S(2)}) copy-start(bf16[2,1,128,2048]{3,2,1,0:T(8,128)(2,1)} %param.10) | copy-start | bytes 3145732
where the time goes:
time: 441 us; the launch traced here: 440 us
  Pallas kernels  416 us (94%)
  local copies, waits for them, and re-layouts  14 us (3%)
  other arithmetic  8.69 us (2%)
    pallas_call x2, Pallas kernels, gather_blocks(): pl.pallas_call(gather_kernel, out_shape=jax.ShapeDtypeStruct(picks.shape...  259 us
    pallas_call x1, Pallas kernels, pair_attention(): pl.pallas_call(functools.partial(pair_kernel, pool_size, block_len), out_...  157 us

commit v1 on v0

--- a/solution.py
+++ b/solution.py
@@ -165,9 +165,10 @@
             num_scalar_prefetch=1,
             grid=(),
             in_specs=[pl.BlockSpec(memory_space=pl.ANY)],
-            out_specs=pl.BlockSpec(memory_space=pl.ANY),
+            out_specs=pl.BlockSpec(memory_space=pltpu.VMEM),
             scratch_shapes=[pltpu.SemaphoreType.DMA(picks.shape)],
         ),
+        compiler_params=pltpu.CompilerParams(vmem_limit_bytes=16 * 1024 * 1024),
     )(picks, flat_store)
 
 
@@ -383,17 +384,19 @@
         attend(0, t, False)
         if n == 0:
             q_step(1, 3)
-    p_step(0, 1)
+        if n == 1:
+            p_step(0, 1)
     for n, t in enumerate(order):
         kv_copy(1, t).wait_recv()
         wait_query(1, t)
         attend(1, t, False)
         if n < 2:
             p_step(0, n + 2)
-    p_step(1, 1)
+        if n == 1:
+            p_step(1, 1)
+    p_step(1, 2)
     finish(0)
-    for step in range(2, pairs):
-        p_step(1, step)
+    p_step(1, 3)
     for d in range(WSLOTS):
         if d:
             back_copy(d).wait_recv()

time: 441 us -> 198 us (0.45)
  Pallas kernels: 416 us -> 172 us
    pallas_call x2, Pallas kernels: 259 us -> 15.1 us  [gather_blocks(): pl.pallas_call(gather_kernel, out_shape=jax.ShapeDtypeStruct(picks.shape...]
where the time goes in v1:
time: 198 us
  Pallas kernels  172 us (87%)
  local copies, waits for them, and re-layouts  15.1 us (8%)
  other arithmetic  8.69 us (4%)
    pallas_call x1, Pallas kernels, pair_attention(): pl.pallas_call(functools.partial(pair_kernel, pool_size, block_len), out_...  157 us
    pallas_call x2, Pallas kernels, gather_blocks(): pl.pallas_call(gather_kernel, out_shape=jax.ShapeDtypeStruct(picks.shape...  15.1 us
    unnamed x16, local copies, waits for them, and re-layouts  6.75 us

profile of v1, /device:TPU:8, one launch (start us, length us, event | category | flops | bytes accessed | tf_op | source)
XLA Modules:
  0.0 197.8 jit_solution(9911597996480692452)
XLA Ops:
  0.7 1.3 dynamic_slice.22
  2.7 0.2 dynamic-slice_reduce_fusion
  3.0 0.7 iota_compare_fusion.3
  3.7 0.3 compare_reduce_fusion.7
  4.0 0.8 fusion.12
  4.8 0.1 convert_reduce_fusion.1
  5.0 0.1 reshape.395
  5.0 0.1 reshape.396
  5.1 0.1 constant_dynamic-slice_fusion.2
  5.2 0.1 copy.62
  5.3 0.6 gather_fusion.1
  5.9 0.1 copy.59
  6.0 0.6 gather_fusion
  6.6 0.1 copy.45
  6.7 0.1 copy.46
  6.8 0.6 pad_add_fusion.counts
  7.4 0.1 convolution_convert_fusion
  7.5 0.4 select_reduce_fusion
  8.0 0.6 gather_fusion.3
  8.6 0.6 gather_fusion.2
  9.2 0.1 reshape.400.picks
  9.3 0.1 reshape.397.picks
  9.4 0.3 multiply_cosine_fusion
  9.7 1.0 reshape_squeeze.2
  10.7 0.4 slice_convert_fusion
  11.1 0.5 fusion
  11.6 0.4 pad_maximum_fusion.5
  11.9 0.3 copy.55
  12.2 0.6 pad_maximum_fusion.4
  12.8 0.1 reshape_reshape.3
  12.9 0.8 reshape.402.new_ref
  13.8 0.1 select_select_fusion.3
  13.9 0.9 pad_maximum_fusion.3.back_ref
  14.8 0.2 convert_bitcast_fusion.1
  15.0 0.2 copy.72
  15.2 0.2 copy.73
  15.4 0.3 fusion.11
  15.7 0.3 fusion.10
  16.1 1.4 subtract_convert_fusion.1
  17.5 0.6 pad_maximum_fusion.1
  18.1 1.1 pad_maximum_fusion.q_ref
  19.1 0.2 slice-done.1
  19.3 7.7 %shard_map.77 = bf16[64,64,512]{2,1,0:T(8,128)(2,1)S(1)} custom-call(s32[64]{0:T(128)S(1)} %reshape.397.picks, bf16[128,64,512]{2,1,0:T(8,128)(2,1)S(1)} %bitcast.88), custom_call_target="tpu_custom_call" | custom-call | tf_op jit(solution)/shard_map/pallas_call | solution.py:161
  27.0 7.5 %shard_map.78 = bf16[64,64,512]{2,1,0:T(8,128)(2,1)S(1)} custom-call(s32[64]{0:T(128)S(1)} %reshape.400.picks, bf16[128,64,512]{2,1,0:T(8,128)(2,1)S(1)} %bitcast.89), custom_call_target="tpu_custom_call" | custom-call | tf_op jit(solution)/shard_map/pallas_call | solution.py:161
  34.5 2.0 copy-done.2
  36.5 157.1 %shard_map.79 = (bf16[2,128,2048]{2,1,0:T(8,128)(2,1)}, bf16[2,4,64,512]{3,2,1,0:T(8,128)(2,1)}) custom-call(s32[2,2,4]{2,1,0:T(2,128)} %pad_add_fusion.counts, bf16[2,2,1024,128]{3,2,1,0:T(8,128)(2,1)} %pad_maximum_fusion.q_ref, bf16[2,4,512,512]{3,2,1,0:T(8,128)(2,1)} %bitcast.90, bf16[2,4,512,512]{3,2,1,0:T(8,128)(2,1)} %bitcast.91, ...), custom_call_target="tpu_custom_call" | custom-call | tf_op jit(solution)/shard_map/pallas_call | solution.py:429
  193.6 2.3 %copy.84 = bf16[2,1,128,2048]{3,2,1,0:T(8,128)(2,1)} copy(bf16[2,1,128,2048]{3,2,1,0:T(8,128)(2,1)} %bitcast.97) | data formatting | bytes 2097152
  195.9 1.9 copy.85
  (25 shorter events, 0.3 us)
Async XLA Ops:
  0.6 2.1 %copy-start = (s32[2,8,2,2]{1,3,2,0:T(2,128)S(1)}, s32[2,8,2,2]{1,3,2,0:T(2,128)}, u32[]{:S(2)}) copy-start(s32[2,8,2,2]{1,3,2,0:T(2,128)} %param.15) | copy-start | bytes 772
  0.6 14.1 %copy-start.3 = (bf16[2,1,128,2048]{3,2,1,0:T(8,128)(2,1)S(1)}, bf16[2,1,128,2048]{3,2,1,0:T(8,128)(2,1)}, u32[]{:S(2)}) copy-start(bf16[2,1,128,2048]{3,2,1,0:T(8,128)(2,1)} %param.10) | copy-start | bytes 3145732
  15.7 3.4 %slice-start = ((s8[8388608]{0:T(1024)(128)(4,1)}), s8[4194304]{0:T(1024)(128)(4,1)S(1)}, s32[]{:S(2)}) async-start(s8[8388608]{0:T(1024)(128)(4,1)} %bitcast.86), calls=%async_computation | async-start | bytes 8388608
  16.1 3.3 %slice-start.1 = ((s8[8388608]{0:T(1024)(128)(4,1)}), s8[4194304]{0:T(1024)(128)(4,1)S(1)}, s32[]{:S(2)}) async-start(s8[8388608]{0:T(1024)(128)(4,1)} %bitcast.86), calls=%async_computation.1 | async-start | bytes 8388608
  27.0 7.5 %copy-start.1 = (bf16[64,64,512]{2,1,0:T(8,128)(2,1)}, bf16[64,64,512]{2,1,0:T(8,128)(2,1)S(1)}, u32[]{:S(2)}) copy-start(bf16[64,64,512]{2,1,0:T(8,128)(2,1)S(1)} %shard_map.77) | copy-start | bytes 12582916
  34.5 2.0 copy-start.2
